TPU v7x, 128 devices: a whole 4x4x4 slice. The times are simulated.
128 devices in a mesh: dp: 16 (over x_hi, y, core), tensor: 8 (over z, x_lo).
Axes of the slice: x: 4 (x_hi: 2, x_lo: 2; x = x_hi * 2 + x_lo), y: 4, z: 4, core: 2. Of those that a mesh axis runs over, the one named last changes fastest.
Arguments:
- hidden_in: bfloat16 [16384, 1024], P(('dp', 'tensor')), may hold values from -6 to 6
- segment_ids: int32 [16384], P(('dp', 'tensor')), may hold values from -1 to 129, as said below
- w_qkv: bfloat16 [2, 1024, 3, 1024], P(None, 'dp', None, 'tensor'), may hold values from -0.1875 to 0.1875
- b_qv: float32 [2, 2, 1024], P(None, None, 'tensor'), may hold values from -3 to 3
- w_out: bfloat16 [2, 1024, 1024], P(None, 'tensor', 'dp'), may hold values from -1.5 to 1.5
- b_out: float32 [2, 1024], replicated, may hold values from -2 to 2
- ln1_gain: float32 [2, 1024], replicated, may hold values from 0.5 to 1.5
- ln1_bias: float32 [2, 1024], replicated, may hold values from -2 to 2
- w_up: bfloat16 [2, 1024, 4096], P(None, 'dp', 'tensor'), may hold values from -0.1875 to 0.1875
- b_up: float32 [2, 4096], P(None, 'tensor'), may hold values from -3 to 3
- w_down: bfloat16 [2, 4096, 1024], P(None, 'tensor', 'dp'), may hold values from -0.125 to 0.125
- b_down: float32 [2, 1024], replicated, may hold values from -2 to 2
- ln2_gain: float32 [2, 1024], replicated, may hold values from 0.5 to 1.5
- ln2_bias: float32 [2, 1024], replicated, may hold values from -2 to 2
- out_grad: bfloat16 [16384, 1024], P(('dp', 'tensor')), may hold values from -6 to 6
Outputs:
- hidden_out: bfloat16 [16384, 1024], P(('dp', 'tensor'))
- hidden_grad: float32 [16384, 1024], P(('dp', 'tensor'))
- grad_w_qkv: float32 [2, 1024, 3, 1024], P(None, 'dp', None, 'tensor')
- grad_b_qv: float32 [2, 2, 1024], P(None, None, 'tensor')
- grad_w_out: float32 [2, 1024, 1024], P(None, 'tensor', 'dp')
- grad_b_out: float32 [2, 1024], replicated
- grad_ln1_gain: float32 [2, 1024], replicated
- grad_ln1_bias: float32 [2, 1024], replicated
- grad_w_up: float32 [2, 1024, 4096], P(None, 'dp', 'tensor')
- grad_b_up: float32 [2, 4096], P(None, 'tensor')
- grad_w_down: float32 [2, 4096, 1024], P(None, 'tensor', 'dp')
- grad_b_down: float32 [2, 1024], replicated
- grad_ln2_gain: float32 [2, 1024], replicated
- grad_ln2_bias: float32 [2, 1024], replicated
Inputs may be any that keep to these rules, and one draw needn't show every extreme that they name: `segment_ids`: in each group of 1024 slots: zero or more short documents, then one document with id 128 + 1 that starts within the group's first 128 slots and ends within its last 128 slots, then one or more empty slots (-1). Document ids are compared only for equality.
All inputs are finite; a program needn't handle non-finite values.
Results may differ from a plain program's by a relative error of at most 0.023.
Values may be sent and summed in bfloat16 or wider, within the bound.
No kernel may reach another device: no remote copies, remote signals or barrier semaphores. Data moves between devices by JAX's collectives and lax.ppermute only.
A program may use at most 128 MiB of HBM per device.

v0:
```python
import jax
import jax.numpy as jnp
from jax import lax
from jax.sharding import PartitionSpec as P

HEAD_DIM = 64


eps = 1e-05
big_negative = -1e30


def norm_rows(values, scale_vec, shift_vec):
    center = values - jnp.mean(values, axis=-1, keepdims=True)
    spread = jnp.mean(center * center, axis=-1, keepdims=True)
    return center * lax.rsqrt(spread + eps) * scale_vec + shift_vec


def gelu_tanh(values):
    return jax.nn.gelu(values, approximate=True)


def allowed_pairs(seg_rows, seg_cols, row_first):
    shape_pair = (seg_rows.shape[0], seg_cols.shape[0])
    row_pos = row_first + lax.broadcasted_iota(jnp.int32, shape_pair, 0)
    col_pos = lax.broadcasted_iota(jnp.int32, shape_pair, 1)
    same_doc = (
        (seg_rows[:, None] == seg_cols[None, :]) & (seg_rows[:, None] >= 0) & (col_pos <= row_pos)
    )
    return same_doc | (col_pos == row_pos)


def split_heads(qkv_lo):
    group_rows, _, head_cols = qkv_lo.shape
    head_count = head_cols // HEAD_DIM
    queries = qkv_lo[:, 0].reshape(group_rows, head_count, HEAD_DIM)
    keys_all = qkv_lo[:, 1].reshape(group_rows, head_count, HEAD_DIM)
    values_all = qkv_lo[:, 2].reshape(group_rows, head_count, HEAD_DIM)
    return (queries, keys_all, values_all)


def block_scores(queries, keys_all, seg_full, row_first, key_end):
    scores = jnp.einsum(
        "qhd,khd->hqk",
        queries[row_first:key_end],
        keys_all[:key_end],
        preferred_element_type=jnp.float32,
    ) * HEAD_DIM ** (-0.5)
    allowed = allowed_pairs(seg_full[row_first:key_end], seg_full[:key_end], row_first)
    return jnp.where(allowed[None], scores, big_negative)


def attend_forward(qkv_lo, seg_full, block_rows):
    group_rows, _, head_cols = qkv_lo.shape
    queries, keys_all, values_all = split_heads(qkv_lo)
    mixed_rows = []
    log_totals = []
    for block_at in range(group_rows // block_rows):
        row_first = block_at * block_rows
        key_end = row_first + block_rows
        scores = block_scores(queries, keys_all, seg_full, row_first, key_end)
        row_top = jnp.max(scores, axis=-1, keepdims=True)
        log_total = row_top + jnp.log(jnp.sum(jnp.exp(scores - row_top), axis=-1, keepdims=True))
        attn_prob = jnp.exp(scores - log_total).astype(jnp.bfloat16)
        mixed = jnp.einsum(
            "hqk,khd->qhd", attn_prob, values_all[:key_end], preferred_element_type=jnp.float32
        )
        mixed_rows.append(mixed.reshape(block_rows, head_cols).astype(jnp.bfloat16))
        log_totals.append(log_total)
    return (jnp.concatenate(mixed_rows, axis=0), log_totals)


def attend_backward(qkv_lo, seg_full, log_totals, grad_mixed, block_rows):
    group_rows, _, head_cols = qkv_lo.shape
    head_count = head_cols // HEAD_DIM
    score_scale = HEAD_DIM ** (-0.5)
    queries, keys_all, values_all = split_heads(qkv_lo)
    grad_heads = grad_mixed.reshape(group_rows, head_count, HEAD_DIM)
    grad_keys = jnp.zeros((group_rows, head_count, HEAD_DIM), jnp.float32)
    grad_values = jnp.zeros((group_rows, head_count, HEAD_DIM), jnp.float32)
    grad_queries = []
    for block_at in range(group_rows // block_rows):
        row_first = block_at * block_rows
        key_end = row_first + block_rows
        scores = block_scores(queries, keys_all, seg_full, row_first, key_end)
        attn_prob = jnp.exp(scores - log_totals[block_at])
        grad_block = grad_heads[row_first:key_end]
        grad_prob = jnp.einsum(
            "qhd,khd->hqk", grad_block, values_all[:key_end], preferred_element_type=jnp.float32
        )
        grad_scores = attn_prob * (
            grad_prob - jnp.sum(attn_prob * grad_prob, axis=-1, keepdims=True)
        )
        grad_scores = grad_scores.astype(jnp.bfloat16)
        grad_queries.append(
            jnp.einsum(
                "hqk,khd->qhd", grad_scores, keys_all[:key_end], preferred_element_type=jnp.float32
            )
            * score_scale
        )
        grad_keys = grad_keys.at[:key_end].add(
            jnp.einsum(
                "hqk,qhd->khd",
                grad_scores,
                queries[row_first:key_end],
                preferred_element_type=jnp.float32,
            )
            * score_scale
        )
        grad_values = grad_values.at[:key_end].add(
            jnp.einsum(
                "hqk,qhd->khd",
                attn_prob.astype(jnp.bfloat16),
                grad_block,
                preferred_element_type=jnp.float32,
            )
        )
    stacked = jnp.stack([jnp.concatenate(grad_queries, axis=0), grad_keys, grad_values], axis=1)
    return stacked.reshape(group_rows, 3, head_cols).astype(jnp.bfloat16)


def spread_rows(rows_lo, segment_ids):
    return (
        lax.all_gather(rows_lo, "tensor", axis=0, tiled=True),
        lax.all_gather(segment_ids, "tensor", axis=0, tiled=True),
    )


def collect_rows(partials):
    return lax.psum_scatter(
        partials.astype(jnp.bfloat16), "tensor", scatter_dimension=0, tiled=True
    ).astype(jnp.float32)


def spread_grad(grad_lo):
    return lax.all_gather(grad_lo, "tensor", axis=0, tiled=True)


def collect_grad(partials):
    return lax.psum_scatter(
        partials.astype(jnp.bfloat16), "tensor", scatter_dimension=0, tiled=True
    ).astype(jnp.float32)


def local(
    hidden_in,
    segment_ids,
    w_qkv,
    b_qv,
    w_out,
    b_out,
    ln1_gain,
    ln1_bias,
    w_up,
    b_up,
    w_down,
    b_down,
    ln2_gain,
    ln2_bias,
    out_grad,
):
    layer_count = w_qkv.shape[0]
    head_cols = w_qkv.shape[3]
    resid = hidden_in.astype(jnp.float32)
    saved = []
    for layer_at in range(layer_count):
        fetched = (
            lax.all_gather(w_qkv[layer_at], "dp", axis=0, tiled=True),
            lax.all_gather(w_out[layer_at], "dp", axis=1, tiled=True),
            lax.all_gather(w_up[layer_at], "dp", axis=0, tiled=True),
            lax.all_gather(w_down[layer_at], "dp", axis=1, tiled=True),
        )
        qkv_full, out_full, up_full, down_full = fetched
        model_width = qkv_full.shape[0]
        normed = norm_rows(resid, ln1_gain[layer_at], ln1_bias[layer_at]).astype(jnp.bfloat16)
        normed_full, seg_full = spread_rows(normed, segment_ids)
        group_rows = normed_full.shape[0]
        block_rows = min(512, group_rows)
        pre_qkv = jnp.dot(
            normed_full,
            qkv_full.reshape(model_width, 3 * head_cols),
            preferred_element_type=jnp.float32,
        )
        zero_bias = jnp.zeros_like(b_qv[layer_at, 0])
        qkv_bias = jnp.stack([b_qv[layer_at, 0], zero_bias, b_qv[layer_at, 1]])
        qkv_lo = (pre_qkv.reshape(group_rows, 3, head_cols) + qkv_bias[None]).astype(jnp.bfloat16)
        mixed_lo, log_totals = attend_forward(qkv_lo, seg_full, block_rows)
        branch = collect_rows(jnp.dot(mixed_lo, out_full, preferred_element_type=jnp.float32))
        resid_mid = resid + branch + b_out[layer_at]
        cnorm = norm_rows(resid_mid, ln2_gain[layer_at], ln2_bias[layer_at]).astype(jnp.bfloat16)
        cnorm_full, _ = spread_rows(cnorm, segment_ids)
        pre_up = jnp.dot(cnorm_full, up_full, preferred_element_type=jnp.float32) + b_up[layer_at]
        act_lo = gelu_tanh(pre_up).astype(jnp.bfloat16)
        branch = collect_rows(jnp.dot(act_lo, down_full, preferred_element_type=jnp.float32))
        saved.append(
            (
                resid,
                normed_full,
                seg_full,
                qkv_lo,
                mixed_lo,
                log_totals,
                resid_mid,
                cnorm_full,
                pre_up,
                act_lo,
            )
        )
        resid = resid_mid + branch + b_down[layer_at]
    hidden_out = resid.astype(jnp.bfloat16)
    grad_resid = out_grad.astype(jnp.float32)
    big_grads = [None] * layer_count
    head_grads = [None] * layer_count
    unit_grads = [None] * layer_count
    shared_grads = [None] * layer_count
    for layer_at in reversed(range(layer_count)):
        (
            resid_in,
            normed_full,
            seg_full,
            qkv_lo,
            mixed_lo,
            log_totals,
            resid_mid,
            cnorm_full,
            pre_up,
            act_lo,
        ) = saved[layer_at]
        qkv_full, out_full, up_full, down_full = (
            lax.all_gather(w_qkv[layer_at], "dp", axis=0, tiled=True),
            lax.all_gather(w_out[layer_at], "dp", axis=1, tiled=True),
            lax.all_gather(w_up[layer_at], "dp", axis=0, tiled=True),
            lax.all_gather(w_down[layer_at], "dp", axis=1, tiled=True),
        )
        model_width = qkv_full.shape[0]
        group_rows = normed_full.shape[0]
        block_rows = min(512, group_rows)
        grad_low = grad_resid.astype(jnp.bfloat16)
        grad_bdown = jnp.sum(grad_low.astype(jnp.float32), axis=0)
        grad_full = spread_grad(grad_low)
        grad_wdown = jnp.einsum("gf,gd->fd", act_lo, grad_full, preferred_element_type=jnp.float32)
        grad_act = jnp.einsum("gd,fd->gf", grad_full, down_full, preferred_element_type=jnp.float32)
        _, gelu_pull = jax.vjp(gelu_tanh, pre_up)
        grad_pre = gelu_pull(grad_act)[0].astype(jnp.bfloat16)
        grad_bup = jnp.sum(grad_pre.astype(jnp.float32), axis=0)
        grad_wup = jnp.einsum("gd,gf->df", cnorm_full, grad_pre, preferred_element_type=jnp.float32)
        grad_cnorm = collect_grad(
            jnp.einsum("gf,df->gd", grad_pre, up_full, preferred_element_type=jnp.float32)
        )
        _, norm_pull = jax.vjp(norm_rows, resid_mid, ln2_gain[layer_at], ln2_bias[layer_at])
        grad_x, grad_g2, grad_s2 = norm_pull(grad_cnorm)
        grad_resid = grad_resid + grad_x
        grad_low = grad_resid.astype(jnp.bfloat16)
        grad_bout = jnp.sum(grad_low.astype(jnp.float32), axis=0)
        grad_full = spread_grad(grad_low)
        grad_wout = jnp.einsum("gc,gd->cd", mixed_lo, grad_full, preferred_element_type=jnp.float32)
        grad_mixed = jnp.einsum(
            "gd,cd->gc", grad_full, out_full, preferred_element_type=jnp.float32
        ).astype(jnp.bfloat16)
        grad_qkv = attend_backward(qkv_lo, seg_full, log_totals, grad_mixed, block_rows)
        qkv_sums = jnp.sum(grad_qkv.astype(jnp.float32), axis=0)
        grad_bqv = jnp.stack([qkv_sums[0], qkv_sums[2]])
        grad_flat = grad_qkv.reshape(group_rows, 3 * head_cols)
        grad_wqkv = jnp.einsum(
            "gd,gc->dc", normed_full, grad_flat, preferred_element_type=jnp.float32
        ).reshape(model_width, 3, head_cols)
        grad_normed = collect_grad(
            jnp.einsum(
                "gc,dc->gd",
                grad_flat,
                qkv_full.reshape(model_width, 3 * head_cols),
                preferred_element_type=jnp.float32,
            )
        )
        _, norm_pull = jax.vjp(norm_rows, resid_in, ln1_gain[layer_at], ln1_bias[layer_at])
        grad_x, grad_g1, grad_s1 = norm_pull(grad_normed)
        grad_resid = grad_resid + grad_x
        big_grads[layer_at] = (
            lax.psum_scatter(
                grad_wqkv.astype(jnp.bfloat16), "dp", scatter_dimension=0, tiled=True
            ).astype(jnp.float32),
            lax.psum_scatter(
                grad_wout.astype(jnp.bfloat16), "dp", scatter_dimension=1, tiled=True
            ).astype(jnp.float32),
            lax.psum_scatter(
                grad_wup.astype(jnp.bfloat16), "dp", scatter_dimension=0, tiled=True
            ).astype(jnp.float32),
            lax.psum_scatter(
                grad_wdown.astype(jnp.bfloat16), "dp", scatter_dimension=1, tiled=True
            ).astype(jnp.float32),
        )
        head_grads[layer_at] = grad_bqv
        unit_grads[layer_at] = grad_bup
        shared_grads[layer_at] = (grad_bout, grad_g1, grad_s1, grad_bdown, grad_g2, grad_s2)
    sum_bqv, sum_bup = lax.psum((jnp.stack(head_grads), jnp.stack(unit_grads)), "dp")
    shared_stack = tuple(
        (jnp.stack([shared_grads[at][slot] for at in range(layer_count)]) for slot in range(6))
    )
    sum_bout, sum_g1, sum_s1, sum_bdown, sum_g2, sum_s2 = lax.psum(shared_stack, ("dp", "tensor"))
    grad_w_qkv = jnp.stack([big_grads[at][0] for at in range(layer_count)])
    grad_w_out = jnp.stack([big_grads[at][1] for at in range(layer_count)])
    grad_w_up = jnp.stack([big_grads[at][2] for at in range(layer_count)])
    grad_w_down = jnp.stack([big_grads[at][3] for at in range(layer_count)])
    return (
        hidden_out,
        grad_resid,
        grad_w_qkv,
        sum_bqv,
        grad_w_out,
        sum_bout,
        sum_g1,
        sum_s1,
        grad_w_up,
        sum_bup,
        grad_w_down,
        sum_bdown,
        sum_g2,
        sum_s2,
    )


def solution(mesh):
    in_specs = (
        P(("dp", "tensor"), None),
        P(("dp", "tensor")),
        P(None, "dp", None, "tensor"),
        P(None, None, "tensor"),
        P(None, "tensor", "dp"),
        P(),
        P(),
        P(),
        P(None, "dp", "tensor"),
        P(None, "tensor"),
        P(None, "tensor", "dp"),
        P(),
        P(),
        P(),
        P(("dp", "tensor"), None),
    )
    out_specs = (
        P(("dp", "tensor"), None),
        P(("dp", "tensor"), None),
        P(None, "dp", None, "tensor"),
        P(None, None, "tensor"),
        P(None, "tensor", "dp"),
        P(),
        P(),
        P(),
        P(None, "dp", "tensor"),
        P(None, "tensor"),
        P(None, "tensor", "dp"),
        P(),
        P(),
        P(),
    )
    return jax.shard_map(local, mesh=mesh, in_specs=in_specs, out_specs=out_specs, check_vma=False)
```

profile of v0, /device:TPU:1, one launch (start us, length us, event | category | flops | bytes accessed | tf_op | source)
XLA Modules:
  0.0 1713.9 jit_solution(4142204394732466340)
XLA Ops:
  16.4 31.1 %all-gather = bf16[1,1024,3,128]{3,1,2,0:T(8,128)(2,1)S(1)} all-gather(bf16[1,64,3,128]{3,1,2,0:T(8,128)(2,1)S(1)} %get-tuple-element.205), channel_id=2, replica_groups=mesh['dp'=16,'tensor'=8] {'dp'}, dimensions={1}, use_global_device_ids=true | all-gather | bytes 835584 | tf_op jit(solution)/shard_map/all_gather | solution.py:168
  47.9 16.0 all-gather.8
  64.5 22.6 %all-gather.1 = bf16[1,128,1024]{1,2,0:T(8,128)(2,1)S(1)} all-gather(bf16[1,128,64]{1,2,0:T(8,128)(2,1)S(1)} %get-tuple-element.207), channel_id=3, replica_groups=mesh['dp'=16,'tensor'=8] {'dp'}, dimensions={2}, use_global_device_ids=true | all-gather | bytes 278528 | tf_op jit(solution)/shard_map/all_gather | solution.py:169
  104.1 49.6 %reduce-scatter.17.cloned.1.call-done = bf16[128,1024]{1,0:T(8,128)(2,1)} async-done(((bf16[1024,1024]{1,0:T(8,128)(2,1)}), bf16[128,1024]{1,0:T(8,128)(2,1)}) %reduce-scatter.17.cloned.1.call-update) | async-done | bytes 262160 | tf_op jit(solution)/shard_map/reduce_scatter | solution.py:130
  159.4 49.5 %all-gather.24.cloned.1.call-done = bf16[1024,1024]{1,0:T(8,128)(2,1)} async-done(((bf16[128,1024]{1,0:T(8,128)(2,1)}), bf16[1024,1024]{1,0:T(8,128)(2,1)}) %all-gather.24.cloned.1.call-update) | async-done | bytes 2097168 | tf_op jit(solution)/shard_map/all_gather | solution.py:124
  213.4 43.4 %all-gather.40.cloned.1.call-done = bf16[1,512,1024]{1,2,0:T(8,128)(2,1)} async-done(((bf16[1,512,64]{1,2,0:T(8,128)(2,1)}), bf16[1,512,1024]{1,2,0:T(8,128)(2,1)}) %all-gather.40.cloned.1.call-update) | async-done | bytes 1048592 | tf_op jit(solution)/shard_map/all_gather | solution.py:171
  262.7 49.6 %reduce-scatter.19.cloned.1.call-done = bf16[128,1024]{1,0:T(8,128)(2,1)} async-done(((bf16[1024,1024]{1,0:T(8,128)(2,1)}), bf16[128,1024]{1,0:T(8,128)(2,1)}) %reduce-scatter.19.cloned.1.call-update) | async-done | bytes 262160 | tf_op jit(solution)/shard_map/reduce_scatter | solution.py:130
  316.5 31.7 %all-gather.4 = bf16[1,1024,3,128]{3,1,2,0:T(8,128)(2,1)} all-gather(bf16[1,64,3,128]{3,1,2,0:T(8,128)(2,1)} %get-tuple-element.204), channel_id=6, replica_groups=mesh['dp'=16,'tensor'=8] {'dp'}, dimensions={1}, use_global_device_ids=true | all-gather | bytes 835584 | tf_op jit(solution)/shard_map/all_gather | solution.py:168
  350.5 22.9 %all-gather.5 = bf16[1,128,1024]{1,2,0:T(8,128)(2,1)} all-gather(bf16[1,128,64]{1,2,0:T(8,128)(2,1)} %get-tuple-element.206), channel_id=7, replica_groups=mesh['dp'=16,'tensor'=8] {'dp'}, dimensions={2}, use_global_device_ids=true | all-gather | bytes 278528 | tf_op jit(solution)/shard_map/all_gather | solution.py:169
  386.2 53.2 %reduce-scatter.21.cloned.1.call-done = bf16[128,1024]{1,0:T(8,128)(2,1)} async-done(((bf16[1024,1024]{1,0:T(8,128)(2,1)}), bf16[128,1024]{1,0:T(8,128)(2,1)}) %reduce-scatter.21.cloned.1.call-update) | async-done | bytes 262160 | tf_op jit(solution)/shard_map/reduce_scatter | solution.py:130
  444.8 49.6 %all-gather.28.cloned.1.call-done = bf16[1024,1024]{1,0:T(8,128)(2,1)} async-done(((bf16[128,1024]{1,0:T(8,128)(2,1)}), bf16[1024,1024]{1,0:T(8,128)(2,1)}) %all-gather.28.cloned.1.call-update) | async-done | bytes 2097168 | tf_op jit(solution)/shard_map/all_gather | solution.py:124
  498.9 43.3 %all-gather.44.cloned.1.call-done = bf16[1,512,1024]{1,2,0:T(8,128)(2,1)} async-done(((bf16[1,512,64]{1,2,0:T(8,128)(2,1)}), bf16[1,512,1024]{1,2,0:T(8,128)(2,1)}) %all-gather.44.cloned.1.call-update) | async-done | bytes 1048592 | tf_op jit(solution)/shard_map/all_gather | solution.py:171
  542.2 51.6 %all-gather.30.cloned.1.call-done = bf16[1024,1024]{1,0:T(8,128)(2,1)} async-done(((bf16[128,1024]{1,0:T(8,128)(2,1)}), bf16[1024,1024]{1,0:T(8,128)(2,1)}) %all-gather.30.cloned.1.call-update) | async-done | bytes 2097168 | tf_op jit(solution)/shard_map/all_gather | solution.py:136
  608.1 47.5 %reduce-scatter.25.cloned.1.call-done = bf16[128,1024]{1,0:T(8,128)(2,1)} async-done(((bf16[1024,1024]{1,0:T(8,128)(2,1)}), bf16[128,1024]{1,0:T(8,128)(2,1)}) %reduce-scatter.25.cloned.1.call-update) | async-done | bytes 262160 | tf_op jit(solution)/shard_map/reduce_scatter | solution.py:140
  658.8 51.0 %reduce-scatter.23.cloned.1.call-done = bf16[128,1024]{1,0:T(8,128)(2,1)} async-done(((bf16[1024,1024]{1,0:T(8,128)(2,1)}), bf16[128,1024]{1,0:T(8,128)(2,1)}) %reduce-scatter.23.cloned.1.call-update) | async-done | bytes 262160 | tf_op jit(solution)/shard_map/reduce_scatter | solution.py:130
  715.6 50.6 %all-gather.32.cloned.1.call-done = bf16[1024,1024]{1,0:T(8,128)(2,1)} async-done(((bf16[128,1024]{1,0:T(8,128)(2,1)}), bf16[1024,1024]{1,0:T(8,128)(2,1)}) %all-gather.32.cloned.1.call-update) | async-done | bytes 2097168 | tf_op jit(solution)/shard_map/all_gather | solution.py:136
  798.7 52.3 %reduce-scatter.27.cloned.1.call-done = bf16[128,1024]{1,0:T(8,128)(2,1)} async-done(((bf16[1024,1024]{1,0:T(8,128)(2,1)}), bf16[128,1024]{1,0:T(8,128)(2,1)}) %reduce-scatter.27.cloned.1.call-update) | async-done | bytes 262160 | tf_op jit(solution)/shard_map/reduce_scatter | solution.py:140
  858.6 50.9 %all-gather.34.cloned.1.call-done = bf16[1024,1024]{1,0:T(8,128)(2,1)} async-done(((bf16[128,1024]{1,0:T(8,128)(2,1)}), bf16[1024,1024]{1,0:T(8,128)(2,1)}) %all-gather.34.cloned.1.call-update) | async-done | bytes 2097168 | tf_op jit(solution)/shard_map/all_gather | solution.py:136
  909.4 5.7 convert_reduce_fusion.1
  918.8 52.3 %reduce-scatter.29.cloned.1.call-done = bf16[128,1024]{1,0:T(8,128)(2,1)} async-done(((bf16[1024,1024]{1,0:T(8,128)(2,1)}), bf16[128,1024]{1,0:T(8,128)(2,1)}) %reduce-scatter.29.cloned.1.call-update) | async-done | bytes 262160 | tf_op jit(solution)/shard_map/reduce_scatter | solution.py:140
  999.0 29.7 %all-gather.36.cloned.1.call-done = bf16[1024,1024]{1,0:T(8,128)(2,1)} async-done(((bf16[128,1024]{1,0:T(8,128)(2,1)}), bf16[1024,1024]{1,0:T(8,128)(2,1)}) %all-gather.36.cloned.1.call-update) | async-done | bytes 2097168 | tf_op jit(solution)/shard_map/all_gather | solution.py:136
  1064.2 32.9 %reduce-scatter.47.cloned.1.call-done = bf16[512,64]{0,1:T(8,128)(2,1)} async-done(((bf16[512,1024]{0,1:T(8,128)(2,1)}), bf16[512,64]{0,1:T(8,128)(2,1)}) %reduce-scatter.47.cloned.1.call-update) | async-done | bytes 65552 | tf_op jit(solution)/shard_map/reduce_scatter | solution.py:288
  1097.1 69.9 %reduce-scatter.45.cloned.1.call-done = bf16[512,64]{0,1:T(8,128)(2,1)} async-done(((bf16[512,1024]{0,1:T(8,128)(2,1)}), bf16[512,64]{0,1:T(8,128)(2,1)}) %reduce-scatter.45.cloned.1.call-update) | async-done | bytes 65552 | tf_op jit(solution)/shard_map/reduce_scatter | solution.py:288
  1168.6 68.0 %reduce-scatter.43.cloned.1.call-done = bf16[64,512]{1,0:T(8,128)(2,1)} async-done(((bf16[1024,512]{1,0:T(8,128)(2,1)}), bf16[64,512]{1,0:T(8,128)(2,1)}) %reduce-scatter.43.cloned.1.call-update) | async-done | bytes 65552 | tf_op jit(solution)/shard_map/reduce_scatter | solution.py:285
  1236.6 70.1 %reduce-scatter.41.cloned.1.call-done = bf16[64,512]{1,0:T(8,128)(2,1)} async-done(((bf16[1024,512]{1,0:T(8,128)(2,1)}), bf16[64,512]{1,0:T(8,128)(2,1)}) %reduce-scatter.41.cloned.1.call-update) | async-done | bytes 65552 | tf_op jit(solution)/shard_map/reduce_scatter | solution.py:285
  1308.4 36.3 %all-reduce.5 = (f32[2,2,128]{2,1,0:T(2,128)}, f32[2,512]{1,0:T(2,128)}) all-reduce(f32[2,2,128]{2,1,0:T(2,128)S(1)} %pad_maximum_fusion.17, f32[2,512]{1,0:T(2,128)S(1)} %pad_maximum_fusion.14), channel_id=1, replica_groups=mesh['dp'=16,'tensor'=8] {'dp'}, use_global_device_ids=true, to_apply=%region_40.41 | all-reduce | flops 1536 | bytes 12288 | tf_op jit(solution)/shard_map/psum | solution.py:295
  1344.7 29.8 %reduce-scatter.39.cloned.1.call-done = bf16[128,64]{0,1:T(8,128)(2,1)} async-done(((bf16[128,1024]{0,1:T(8,128)(2,1)}), bf16[128,64]{0,1:T(8,128)(2,1)}) %reduce-scatter.39.cloned.1.call-update) | async-done | bytes 16400 | tf_op jit(solution)/shard_map/reduce_scatter | solution.py:282
  1374.5 67.8 %reduce-scatter.37.cloned.1.call-done = bf16[128,64]{0,1:T(8,128)(2,1)} async-done(((bf16[128,1024]{0,1:T(8,128)(2,1)}), bf16[128,64]{0,1:T(8,128)(2,1)}) %reduce-scatter.37.cloned.1.call-update) | async-done | bytes 16400 | tf_op jit(solution)/shard_map/reduce_scatter | solution.py:282
  1443.7 67.4 %reduce-scatter.35.cloned.1.call-done = bf16[64,3,128]{2,0,1:T(8,128)(2,1)} async-done(((bf16[1024,3,128]{2,0,1:T(8,128)(2,1)}), bf16[64,3,128]{2,0,1:T(8,128)(2,1)}) %reduce-scatter.35.cloned.1.call-update) | async-done | bytes 49168 | tf_op jit(solution)/shard_map/reduce_scatter | solution.py:279
  1511.1 69.2 %reduce-scatter.33.cloned.1.call-done = bf16[64,3,128]{2,0,1:T(8,128)(2,1)} async-done(((bf16[1024,3,128]{2,0,1:T(8,128)(2,1)}), bf16[64,3,128]{2,0,1:T(8,128)(2,1)}) %reduce-scatter.33.cloned.1.call-update) | async-done | bytes 49168 | tf_op jit(solution)/shard_map/reduce_scatter | solution.py:279
  1581.8 54.2 %reduce-scatter.31.cloned.1.call-done = bf16[128,1024]{1,0:T(8,128)(2,1)} async-done(((bf16[1024,1024]{1,0:T(8,128)(2,1)}), bf16[128,1024]{1,0:T(8,128)(2,1)}) %reduce-scatter.31.cloned.1.call-update) | async-done | bytes 262160 | tf_op jit(solution)/shard_map/reduce_scatter | solution.py:140
  1638.6 65.2 %all-reduce.4 = (f32[2,1024]{1,0:T(2,128)}, f32[2,1024]{1,0:T(2,128)}, f32[2,1024]{1,0:T(2,128)}, f32[2,1024]{1,0:T(2,128)}, f32[2,1024]{1,0:T(2,128)}, /*index=5*/f32[2,1024]{1,0:T(2,128)}) all-reduce(f32[2,1024]{1,0:T(2,128)S(1)} %get-tuple-element.256, ...), channel_id=1, replica_groups=mesh['dp'=16,'tensor'=8] {'dp','tensor'}, use_global_device_ids=true, to_apply=%region_45.46 | all-reduce | flops 12288 | bytes 98304 | tf_op jit(solution)/shard_map/psum | solution.py:299
  (441 shorter events, 211.6 us)
Async XLA Ops:
  8.0 81.7 %all-gather.22.cloned.1.call-start = ((), (), s32[]{:S(2)}) async-start(), calls=%async_computation.16 | async-start | bytes 2359296 | tf_op jit(solution)/shard_map/all_gather | solution.py:124
  14.9 138.7 %reduce-scatter.17.cloned.1.call-start = ((), (), s32[]{:S(2)}) async-start(), calls=%async_computation.17 | async-start | bytes 2359296 | tf_op jit(solution)/shard_map/reduce_scatter | solution.py:130
  101.5 58.0 %all-gather.38.cloned.1.call-start = ((), (), s32[]{:S(2)}) async-start(), calls=%async_computation.40 | async-start | bytes 1114112 | tf_op jit(solution)/shard_map/all_gather | solution.py:170
  102.2 106.7 %all-gather.24.cloned.1.call-start = ((), (), s32[]{:S(2)}) async-start(), calls=%async_computation.18 | async-start | bytes 2359296 | tf_op jit(solution)/shard_map/all_gather | solution.py:124
  157.8 98.9 %all-gather.40.cloned.1.call-start = ((), (), s32[]{:S(2)}) async-start(), calls=%async_computation.41 | async-start | bytes 1114112 | tf_op jit(solution)/shard_map/all_gather | solution.py:171
  158.6 153.7 %reduce-scatter.19.cloned.1.call-start = ((), (), s32[]{:S(2)}) async-start(), calls=%async_computation.19 | async-start | bytes 2359296 | tf_op jit(solution)/shard_map/reduce_scatter | solution.py:130
  261.4 112.0 %all-gather.26.cloned.1.call-start = ((), (), s32[]{:S(2)}) async-start(), calls=%async_computation.20 | async-start | bytes 2359296 | tf_op jit(solution)/shard_map/all_gather | solution.py:124
  316.4 123.0 %reduce-scatter.21.cloned.1.call-start = ((), (), s32[]{:S(2)}) async-start(), calls=%async_computation.21 | async-start | bytes 2359296 | tf_op jit(solution)/shard_map/reduce_scatter | solution.py:130
  385.4 59.4 %all-gather.42.cloned.1.call-start = ((), (), s32[]{:S(2)}) async-start(), calls=%async_computation.42 | async-start | bytes 1114112 | tf_op jit(solution)/shard_map/all_gather | solution.py:170
  386.2 108.2 %all-gather.28.cloned.1.call-start = ((), (), s32[]{:S(2)}) async-start(), calls=%async_computation.22 | async-start | bytes 2359296 | tf_op jit(solution)/shard_map/all_gather | solution.py:124
  443.3 98.9 %all-gather.44.cloned.1.call-start = ((), (), s32[]{:S(2)}) async-start(), calls=%async_computation.43 | async-start | bytes 1114112 | tf_op jit(solution)/shard_map/all_gather | solution.py:171
  443.9 149.9 %all-gather.30.cloned.1.call-start = ((), (), s32[]{:S(2)}) async-start(), calls=%async_computation.24 | async-start | bytes 2359296 | tf_op jit(solution)/shard_map/all_gather | solution.py:136
  444.5 211.2 %reduce-scatter.25.cloned.1.call-start = ((), (), s32[]{:S(2)}) async-start(), calls=%async_computation.25 | async-start | bytes 2359296 | tf_op jit(solution)/shard_map/reduce_scatter | solution.py:140
  603.3 106.5 %reduce-scatter.23.cloned.1.call-start = ((), (), s32[]{:S(2)}) async-start(), calls=%async_computation.23 | async-start | bytes 2359296 | tf_op jit(solution)/shard_map/reduce_scatter | solution.py:130
  608.1 158.1 %all-gather.32.cloned.1.call-start = ((), (), s32[]{:S(2)}) async-start(), calls=%async_computation.26 | async-start | bytes 2359296 | tf_op jit(solution)/shard_map/all_gather | solution.py:136
  715.1 135.9 %reduce-scatter.27.cloned.1.call-start = ((), (), s32[]{:S(2)}) async-start(), calls=%async_computation.27 | async-start | bytes 2359296 | tf_op jit(solution)/shard_map/reduce_scatter | solution.py:140
  798.7 110.8 %all-gather.34.cloned.1.call-start = ((), (), s32[]{:S(2)}) async-start(), calls=%async_computation.28 | async-start | bytes 2359296 | tf_op jit(solution)/shard_map/all_gather | solution.py:136
  858.4 112.8 %reduce-scatter.29.cloned.1.call-start = ((), (), s32[]{:S(2)}) async-start(), calls=%async_computation.29 | async-start | bytes 2359296 | tf_op jit(solution)/shard_map/reduce_scatter | solution.py:140
  918.8 109.9 %all-gather.36.cloned.1.call-start = ((), (), s32[]{:S(2)}) async-start(), calls=%async_computation.30 | async-start | bytes 2359296 | tf_op jit(solution)/shard_map/all_gather | solution.py:136
  977.6 119.5 %reduce-scatter.47.cloned.1.call-start = ((), (), s32[]{:S(2)}) async-start(), calls=%async_computation.39 | async-start | bytes 1114112 | tf_op jit(solution)/shard_map/reduce_scatter | solution.py:288
  982.4 184.7 %reduce-scatter.45.cloned.1.call-start = ((), (), s32[]{:S(2)}) async-start(), calls=%async_computation.38 | async-start | bytes 1114112 | tf_op jit(solution)/shard_map/reduce_scatter | solution.py:288
  987.1 249.5 %reduce-scatter.43.cloned.1.call-start = ((), (), s32[]{:S(2)}) async-start(), calls=%async_computation.37 | async-start | bytes 1114112 | tf_op jit(solution)/shard_map/reduce_scatter | solution.py:285
  991.4 315.4 %reduce-scatter.41.cloned.1.call-start = ((), (), s32[]{:S(2)}) async-start(), calls=%async_computation.36 | async-start | bytes 1114112 | tf_op jit(solution)/shard_map/reduce_scatter | solution.py:285
  995.6 379.0 %reduce-scatter.39.cloned.1.call-start = ((), (), s32[]{:S(2)}) async-start(), calls=%async_computation.35 | async-start | bytes 278528 | tf_op jit(solution)/shard_map/reduce_scatter | solution.py:282
  999.0 443.4 %reduce-scatter.37.cloned.1.call-start = ((), (), s32[]{:S(2)}) async-start(), calls=%async_computation.34 | async-start | bytes 278528 | tf_op jit(solution)/shard_map/reduce_scatter | solution.py:282
  1032.0 479.2 %reduce-scatter.35.cloned.1.call-start = ((), (), s32[]{:S(2)}) async-start(), calls=%async_computation.33 | async-start | bytes 835584 | tf_op jit(solution)/shard_map/reduce_scatter | solution.py:279
  1038.6 541.7 %reduce-scatter.33.cloned.1.call-start = ((), (), s32[]{:S(2)}) async-start(), calls=%async_computation.32 | async-start | bytes 835584 | tf_op jit(solution)/shard_map/reduce_scatter | solution.py:279
  1061.3 574.6 %reduce-scatter.31.cloned.1.call-start = ((), (), s32[]{:S(2)}) async-start(), calls=%async_computation.31 | async-start | bytes 2359296 | tf_op jit(solution)/shard_map/reduce_scatter | solution.py:140
  1064.1 639.7 %copy-start.12 = (f32[128,1024]{1,0:T(8,128)S(1)}, f32[128,1024]{1,0:T(8,128)}, u32[]{:S(2)}) copy-start(f32[128,1024]{1,0:T(8,128)} %get-tuple-element.167) | copy-start | bytes 1572868
  1064.1 639.7 %copy-start.14 = (bf16[128,1024]{1,0:T(8,128)(2,1)S(1)}, bf16[128,1024]{1,0:T(8,128)(2,1)}, u32[]{:S(2)}) copy-start(bf16[128,1024]{1,0:T(8,128)(2,1)} %reduce-scatter.29.cloned.1.call-done) | copy-start | bytes 786436
  1064.1 639.7 %copy-start.86 = (f32[128]{0:T(128)S(1)}, f32[128]{0:T(128)}, u32[]{:S(2)}) copy-start(f32[128]{0:T(128)} %copy-done.84) | copy-start | bytes 1540
  1064.1 639.6 %copy-start.91 = (f32[128]{0:T(128)S(1)}, f32[128]{0:T(128)}, u32[]{:S(2)}) copy-start(f32[128]{0:T(128)} %copy-done.90) | copy-start | bytes 1540
  (111 other events, 7977.4 us)
Sparse Core Ops, SparseCore 0:
  15.1 57.3 all-gather.21
  101.6 52.0 reduce-scatter.16
  316.5 53.6 all-gather.25
  385.6 53.7 reduce-scatter.20
  603.4 52.2 reduce-scatter.24
  657.9 51.7 reduce-scatter.22
  798.8 52.1 reduce-scatter.26
  918.9 52.1 reduce-scatter.28
Sparse Core Ops, SparseCore 1:
  105.0 45.6 all-gather.37
  157.9 50.9 all-gather.23
  211.8 44.8 all-gather.39
  261.5 50.7 reduce-scatter.18
  389.3 47.0 all-gather.41
  443.4 50.9 all-gather.27
  497.3 44.8 all-gather.43
  543.7 50.1 all-gather.29
  715.2 50.9 all-gather.31
  858.4 50.9 all-gather.33
  977.7 50.9 all-gather.35
  1032.5 64.6 reduce-scatter.46
  1101.2 65.8 reduce-scatter.44
  1170.8 65.7 reduce-scatter.42
  1240.9 65.8 reduce-scatter.40
  1310.4 64.1 reduce-scatter.38
  1378.2 64.0 reduce-scatter.36
  1446.1 64.9 reduce-scatter.34
  1515.3 65.0 reduce-scatter.32
  1582.7 53.2 reduce-scatter.30
where the time goes:
time: 1720 us; the launch traced here: 1710 us
  waiting for transfers between devices  1260 us (73%)
  blocking collectives  226 us (13%)
  matrix products  115 us (7%)
  other arithmetic  61.4 us (4%)
  local copies, waits for them, and re-layouts  35.8 us (2%)
  between operations  17.7 us (1%)
    reduce_scatter x4, waiting for transfers between devices, collect_grad(): lax.psum_scatter(partials.astype(jnp.bfloat16), 'tensor', scatter_dimensi...  206 us
    reduce_scatter x4, waiting for transfers between devices, collect_rows(): lax.psum_scatter(partials.astype(jnp.bfloat16), 'tensor', scatter_dimensi...  203 us
    all_gather x4, waiting for transfers between devices, spread_grad(): return lax.all_gather(grad_lo, 'tensor', axis=0, tiled=True)  183 us
    reduce_scatter x2, waiting for transfers between devices, local(): lax.psum_scatter(grad_wup.astype(jnp.bfloat16), 'dp', scatter_dimension=0...  138 us
    reduce_scatter x2, waiting for transfers between devices, local(): lax.psum_scatter(grad_wqkv.astype(jnp.bfloat16), 'dp', scatter_dimension=...  137 us
    reduce_scatter x2, waiting for transfers between devices, local(): lax.psum_scatter(grad_wdown.astype(jnp.bfloat16), 'dp', scatter_dimension...  103 us
    all_gather x4, waiting for transfers between devices, spread_rows(): lax.all_gather(rows_lo, 'tensor', axis=0, tiled=True)  99 us
    reduce_scatter x2, waiting for transfers between devices, local(): lax.psum_scatter(grad_wout.astype(jnp.bfloat16), 'dp', scatter_dimension=...  97.6 us
  transfers between devices with their start and end apart: 28, of which 24 were waited for; matrix products, arithmetic and copies ran while one was open for 5% of the time, Pallas kernels for 0%

commit v1 on v0

v1 whole, which is shorter than its diff:
```python
import jax
import jax.numpy as jnp
from jax import lax
from jax.experimental import pallas as pl
from jax.experimental.pallas import tpu as pltpu
from jax.sharding import Mesh
from jax.sharding import PartitionSpec as P

HEAD_DIM = 64
eps = 1e-05
big_negative = -1e30
score_scale = HEAD_DIM ** (-0.5)

AXES = ("xh", "y", "c", "z", "xl")
PLANE = ("xh", "y", "xl")
PLANE_CORES = ("xh", "y", "xl", "c")
CHUNK = 128


def norm_rows(values, scale_vec, shift_vec):
    center = values - jnp.mean(values, axis=-1, keepdims=True)
    spread = jnp.mean(center * center, axis=-1, keepdims=True)
    return center * lax.rsqrt(spread + eps) * scale_vec + shift_vec


def gelu_tanh(values):
    return jax.nn.gelu(values, approximate=True)


def swap_rows(values):
    return lax.ppermute(values, ("c", "xl"), [(0, 0), (1, 2), (2, 1), (3, 3)])


def other_core(values):
    return lax.ppermute(values, "c", [(0, 1), (1, 0)])


def share(values, axis, count):
    copies = jnp.broadcast_to(values[None], (count,) + values.shape)
    return lax.all_to_all(copies, axis, 0, 0, tiled=True)


def spread_z(rows):
    return share(rows, "z", 4).reshape(4 * rows.shape[0], rows.shape[1])


def collect_z(partials):
    low = partials.astype(jnp.bfloat16)
    chunks = low.reshape(4, low.shape[0] // 4, low.shape[1])
    arrived = lax.all_to_all(chunks, "z", 0, 0, tiled=True)
    return jnp.sum(arrived.astype(jnp.float32), axis=0)


def nt_dot(left, right):
    return lax.dot_general(left, right, (((1,), (1,)), ((), ())), preferred_element_type=jnp.float32)


def nn_dot(left, right):
    return jnp.dot(left, right, preferred_element_type=jnp.float32)


def interleave(own, other):
    pieces = []
    for at in range(own.shape[0] // CHUNK):
        pieces += [own[at * CHUNK : (at + 1) * CHUNK], other[at * CHUNK : (at + 1) * CHUNK]]
    return jnp.concatenate(pieces, axis=0)


def by_head(block):
    first = lax.broadcasted_iota(jnp.int32, block.shape, 1) < HEAD_DIM
    zero = jnp.zeros_like(block)
    return jnp.concatenate([jnp.where(first, block, zero), jnp.where(first, zero, block)], axis=0)


def pick_heads(both):
    first = lax.broadcasted_iota(jnp.int32, (CHUNK, CHUNK), 0) < HEAD_DIM
    return jnp.where(first, both[:, :CHUNK], both[:, CHUNK:]).T


def tile_mask(keys_ref, rows_ref, at):
    key_count = 2 * CHUNK * (at + 1)
    seg_keys, pos_keys = keys_ref[0, :key_count], keys_ref[1, :key_count]
    seg_rows = rows_ref[0:1, at * CHUNK : (at + 1) * CHUNK]
    pos_rows = rows_ref[1:2, at * CHUNK : (at + 1) * CHUNK]
    allowed = ((seg_keys == seg_rows) & (seg_rows >= 0) & (pos_keys <= pos_rows)) | (
        pos_keys == pos_rows
    )
    bias = jnp.where(allowed, 0.0, big_negative)
    return jnp.concatenate([bias, bias], axis=1)


def masked_scores(keys_all, q_heads, bias):
    scores = nt_dot(keys_all, q_heads) * score_scale
    return jnp.where(bias < 0.0, big_negative, scores)


def forward_kernel(qkv_ref, kv_ref, keys_ref, rows_ref, mixed_ref, lse_ref):
    tiles = qkv_ref.shape[0] // CHUNK
    biases = [tile_mask(keys_ref, rows_ref, at) for at in range(tiles)]
    for block in range(2):
        base = block * 3 * CHUNK
        k_own = qkv_ref[:, base + CHUNK : base + 2 * CHUNK]
        v_own = qkv_ref[:, base + 2 * CHUNK : base + 3 * CHUNK]
        k_other = kv_ref[:, block * 2 * CHUNK : block * 2 * CHUNK + CHUNK]
        v_other = kv_ref[:, block * 2 * CHUNK + CHUNK : block * 2 * CHUNK + 2 * CHUNK]
        keys_all = interleave(k_own, k_other)
        values_t = interleave(v_own, v_other).T
        for at in range(tiles):
            rows = slice(at * CHUNK, (at + 1) * CHUNK)
            count = 2 * CHUNK * (at + 1)
            q_heads = by_head(qkv_ref[rows, base : base + CHUNK])
            scores = masked_scores(keys_all[:count], q_heads, biases[at])
            top = jnp.max(scores, axis=0, keepdims=True)
            expo = jnp.exp(scores - top)
            total = jnp.sum(expo, axis=0, keepdims=True)
            prob = (expo * (1.0 / total)).astype(jnp.bfloat16)
            mixed = pick_heads(nn_dot(values_t[:, :count], prob))
            mixed_ref[rows, block * CHUNK : (block + 1) * CHUNK] = mixed.astype(jnp.bfloat16)
            lse = top + jnp.log(total)
            lse_ref[2 * block : 2 * block + 1, rows] = lse[:, :CHUNK]
            lse_ref[2 * block + 1 : 2 * block + 2, rows] = lse[:, CHUNK:]


def backward_kernel(
    qkv_ref, kv_ref, keys_ref, rows_ref, lse_ref, dmix_ref, dq_ref, own_ref, other_ref, dk_ref, dv_ref
):
    tiles = qkv_ref.shape[0] // CHUNK
    biases = [tile_mask(keys_ref, rows_ref, at) for at in range(tiles)]
    for block in range(2):
        base = block * 3 * CHUNK
        k_own = qkv_ref[:, base + CHUNK : base + 2 * CHUNK]
        v_own = qkv_ref[:, base + 2 * CHUNK : base + 3 * CHUNK]
        k_other = kv_ref[:, block * 2 * CHUNK : block * 2 * CHUNK + CHUNK]
        v_other = kv_ref[:, block * 2 * CHUNK + CHUNK : block * 2 * CHUNK + 2 * CHUNK]
        keys_all = interleave(k_own, k_other)
        values_all = interleave(v_own, v_other)
        keys_t = keys_all.T
        for at in reversed(range(tiles)):
            rows = slice(at * CHUNK, (at + 1) * CHUNK)
            count = 2 * CHUNK * (at + 1)
            q_heads = by_head(qkv_ref[rows, base : base + CHUNK])
            dm_heads = by_head(dmix_ref[rows, block * CHUNK : (block + 1) * CHUNK])
            lse = jnp.concatenate(
                [lse_ref[2 * block : 2 * block + 1, rows], lse_ref[2 * block + 1 : 2 * block + 2, rows]],
                axis=1,
            )
            scores = masked_scores(keys_all[:count], q_heads, biases[at])
            prob = jnp.exp(scores - lse)
            dprob = nt_dot(values_all[:count], dm_heads)
            weighted = jnp.sum(prob * dprob, axis=0, keepdims=True)
            dscore = (prob * (dprob - weighted)).astype(jnp.bfloat16)
            prob_low = prob.astype(jnp.bfloat16)
            dq = pick_heads(nn_dot(keys_t[:, :count], dscore)) * score_scale
            dq_ref[rows, block * CHUNK : (block + 1) * CHUNK] = dq.astype(jnp.bfloat16)
            dk = nn_dot(dscore, q_heads) * score_scale
            dv = nn_dot(prob_low, dm_heads)
            if at == tiles - 1:
                dk_ref[...] = dk
                dv_ref[...] = dv
            else:
                dk_ref[:count] += dk
                dv_ref[:count] += dv
        for at in range(tiles):
            rows = slice(at * CHUNK, (at + 1) * CHUNK)
            mine = slice(2 * at * CHUNK, (2 * at + 1) * CHUNK)
            theirs = slice((2 * at + 1) * CHUNK, (2 * at + 2) * CHUNK)
            k_cols = slice(block * 2 * CHUNK, block * 2 * CHUNK + CHUNK)
            v_cols = slice(block * 2 * CHUNK + CHUNK, block * 2 * CHUNK + 2 * CHUNK)
            own_ref[rows, k_cols] = dk_ref[mine]
            own_ref[rows, v_cols] = dv_ref[mine]
            other_ref[rows, k_cols] = dk_ref[theirs].astype(jnp.bfloat16)
            other_ref[rows, v_cols] = dv_ref[theirs].astype(jnp.bfloat16)


def whole(count):
    return [pl.BlockSpec(memory_space=pltpu.VMEM)] * count


def attend_forward(qkv, kv_other, keys_info, rows_info):
    rows = qkv.shape[0]
    return pl.pallas_call(
        forward_kernel,
        out_shape=(
            jax.ShapeDtypeStruct((rows, 2 * CHUNK), jnp.bfloat16),
            jax.ShapeDtypeStruct((8, rows), jnp.float32),
        ),
        in_specs=whole(4),
        out_specs=tuple(whole(2)),
        compiler_params=pltpu.CompilerParams(vmem_limit_bytes=40 * 1024 * 1024),
        cost_estimate=pl.CostEstimate(flops=700_000_000, bytes_accessed=4_000_000, transcendentals=1_400_000),
        name="attend_forward",
    )(qkv, kv_other, keys_info, rows_info)


def attend_backward(qkv, kv_other, keys_info, rows_info, lse, dmix):
    rows = qkv.shape[0]
    return pl.pallas_call(
        backward_kernel,
        out_shape=(
            jax.ShapeDtypeStruct((rows, 2 * CHUNK), jnp.bfloat16),
            jax.ShapeDtypeStruct((rows, 4 * CHUNK), jnp.float32),
            jax.ShapeDtypeStruct((rows, 4 * CHUNK), jnp.bfloat16),
        ),
        in_specs=whole(6),
        out_specs=tuple(whole(3)),
        scratch_shapes=[
            pltpu.VMEM((2 * rows, CHUNK), jnp.float32),
            pltpu.VMEM((2 * rows, CHUNK), jnp.float32),
        ],
        compiler_params=pltpu.CompilerParams(vmem_limit_bytes=40 * 1024 * 1024),
        cost_estimate=pl.CostEstimate(flops=1_700_000_000, bytes_accessed=6_000_000, transcendentals=1_400_000),
        name="attend_backward",
    )(qkv, kv_other, keys_info, rows_info, lse, dmix)


def quarter(own, other, core):
    slabs, depth, cols = own.shape
    first = core == 0
    own = own.reshape(slabs // 2, 2, depth, cols)
    other = other.reshape(slabs // 2, 2, depth, cols)
    pair = jnp.stack([jnp.where(first, own, other), jnp.where(first, other, own)], axis=1)
    return pair.transpose(0, 1, 3, 2, 4).reshape(slabs * depth, 2, cols)


def core_sum(grad, core):
    depth = 64
    cols = grad.shape[2]
    low = grad.astype(jnp.bfloat16).reshape(8, 2, depth, 2, cols)
    keep = lax.dynamic_index_in_dim(low, core, 1, False).transpose(0, 2, 1, 3)
    give = lax.dynamic_index_in_dim(low, 1 - core, 1, False).transpose(0, 2, 1, 3)
    both = keep.astype(jnp.float32) + other_core(give).astype(jnp.float32)
    return both.astype(jnp.bfloat16).reshape(16, depth, cols)


def norm_pullback(values, gain, shift, grad):
    _, pull = jax.vjp(norm_rows, values, gain, shift)
    return pull(grad)


def local(
    hidden_in,
    segment_ids,
    w_qkv,
    b_qv,
    w_out,
    b_out,
    ln1_gain,
    ln1_bias,
    w_up,
    b_up,
    w_down,
    b_down,
    ln2_gain,
    ln2_bias,
    out_grad,
):
    layer_count = w_qkv.shape[0]
    core = lax.axis_index("c")
    lane = lax.axis_index("xl")

    resid = swap_rows(hidden_in).astype(jnp.float32)

    attn_slab = [
        jnp.concatenate([w_qkv[at].reshape(64, 3 * CHUNK), w_out[at].T], axis=1)
        for at in range(layer_count)
    ]
    feed_slab = [jnp.concatenate([w_up[at], w_down[at].T], axis=1) for at in range(layer_count)]

    def plane_share(slab):
        return share(slab, PLANE, 16)

    def plane_gather(slab):
        return lax.all_gather(slab, PLANE, axis=0)

    gathered_attn = [plane_share(attn_slab[0])]
    gathered_feed = [plane_share(feed_slab[0])]
    later = plane_gather(jnp.concatenate([attn_slab[1], feed_slab[1]], axis=1))
    gathered_attn.append(later[..., : 4 * CHUNK])
    gathered_feed.append(later[..., 4 * CHUNK :])

    seg_pairs = share(segment_ids[None], ("c", "z", "xl"), 16).reshape(2, 4, 2, CHUNK)
    seg_pairs = lax.dynamic_index_in_dim(seg_pairs, lane, 0, False)
    seg_own = lax.dynamic_index_in_dim(seg_pairs, core, 1, False)
    seg_other = lax.dynamic_index_in_dim(seg_pairs, 1 - core, 1, False)
    spots = lax.broadcasted_iota(jnp.int32, (4, CHUNK), 0) * (2 * CHUNK) + lax.broadcasted_iota(
        jnp.int32, (4, CHUNK), 1
    )
    pos_own = spots + core * CHUNK
    pos_other = spots + (1 - core) * CHUNK
    rows_info = jnp.stack([seg_own.reshape(-1), pos_own.reshape(-1)])
    rows_info = jnp.concatenate([rows_info, jnp.zeros((6, 4 * CHUNK), jnp.int32)], axis=0)
    seg_keys = jnp.stack([seg_own, seg_other], axis=1).reshape(8 * CHUNK, 1)
    pos_keys = jnp.stack([pos_own, pos_other], axis=1).reshape(8 * CHUNK, 1)
    keys_info = jnp.broadcast_to(jnp.stack([seg_keys, pos_keys]), (2, 8 * CHUNK, CHUNK))

    bias_mine = jnp.concatenate([b_qv.reshape(layer_count, 2 * CHUNK), b_up], axis=1)
    bias_next = lax.ppermute(bias_mine, "xl", [(0, 1), (1, 0)])
    bias_both = jnp.stack(
        [jnp.where(lane == 0, bias_mine, bias_next), jnp.where(lane == 0, bias_next, bias_mine)], axis=1
    )

    saved = []
    weights = []
    for at in range(layer_count):
        attn_w = quarter(gathered_attn[at], other_core(gathered_attn[at]), core)
        feed_w = quarter(gathered_feed[at], other_core(gathered_feed[at]), core)
        wq = attn_w[..., : 3 * CHUNK].reshape(1024, 6 * CHUNK)
        wo_t = attn_w[..., 3 * CHUNK :].reshape(1024, 2 * CHUNK)
        wu = feed_w[..., :512].reshape(1024, 1024)
        wd_t = feed_w[..., 512:].reshape(1024, 1024)
        weights.append((wq, wo_t, wu, wd_t))
        zero = jnp.zeros((2, CHUNK), jnp.float32)
        qkv_bias = jnp.concatenate(
            [bias_both[at][:, :CHUNK], zero, bias_both[at][:, CHUNK : 2 * CHUNK]], axis=1
        ).reshape(6 * CHUNK)
        up_bias = bias_both[at][:, 2 * CHUNK :].reshape(1024)

        normed = norm_rows(resid, ln1_gain[at], ln1_bias[at]).astype(jnp.bfloat16)
        normed_full = spread_z(normed)
        qkv = (nn_dot(normed_full, wq) + qkv_bias).astype(jnp.bfloat16)
        kv_mine = jnp.concatenate([qkv[:, CHUNK : 3 * CHUNK], qkv[:, 4 * CHUNK :]], axis=1)
        kv_other = other_core(kv_mine)
        mixed, lse = attend_forward(qkv, kv_other, keys_info, rows_info)
        branch = collect_z(nt_dot(mixed, wo_t))
        resid_mid = resid + branch + b_out[at]
        cnorm = norm_rows(resid_mid, ln2_gain[at], ln2_bias[at]).astype(jnp.bfloat16)
        cnorm_full = spread_z(cnorm)
        pre_up = nn_dot(cnorm_full, wu) + up_bias
        act = gelu_tanh(pre_up).astype(jnp.bfloat16)
        branch = collect_z(nt_dot(act, wd_t))
        saved.append((resid, normed_full, qkv, kv_other, mixed, lse, resid_mid, cnorm_full, pre_up, act))
        resid = resid_mid + branch + b_down[at]
    hidden_out = swap_rows(resid.astype(jnp.bfloat16))

    grad = swap_rows(out_grad).astype(jnp.float32)
    shared = [None] * layer_count
    units = [None] * layer_count
    attn_out = [None] * layer_count
    feed_out = [None] * layer_count
    for at in reversed(range(layer_count)):
        resid_in, normed_full, qkv, kv_other, mixed, lse, resid_mid, cnorm_full, pre_up, act = saved[at]
        wq, wo_t, wu, wd_t = weights[at]

        low = grad.astype(jnp.bfloat16)
        g_bdown = jnp.sum(low.astype(jnp.float32), axis=0)
        low_full = spread_z(low)
        d_act = nn_dot(low_full, wd_t)
        _, gelu_pull = jax.vjp(gelu_tanh, pre_up)
        d_pre = gelu_pull(d_act)[0].astype(jnp.bfloat16)
        g_bup = jnp.sum(d_pre.astype(jnp.float32), axis=0)
        d_cnorm = collect_z(nt_dot(d_pre, wu))
        g_wdown = lax.dot_general(
            low_full, act, (((0,), (0,)), ((), ())), preferred_element_type=jnp.float32
        )
        g_wup = lax.dot_general(
            cnorm_full, d_pre, (((0,), (0,)), ((), ())), preferred_element_type=jnp.float32
        )
        feed_sum = core_sum(
            jnp.concatenate([g_wup.reshape(1024, 2, 512), g_wdown.reshape(1024, 2, 512)], axis=2), core
        )
        d_x, g_g2, g_s2 = norm_pullback(resid_mid, ln2_gain[at], ln2_bias[at], d_cnorm)
        grad = grad + d_x

        low = grad.astype(jnp.bfloat16)
        g_bout = jnp.sum(low.astype(jnp.float32), axis=0)
        low_full = spread_z(low)
        d_mix = nn_dot(low_full, wo_t).astype(jnp.bfloat16)
        d_q, d_own, d_other = attend_backward(qkv, kv_other, keys_info, rows_info, lse, d_mix)
        d_kv = (d_own + other_core(d_other).astype(jnp.float32)).astype(jnp.bfloat16)
        d_qkv = jnp.concatenate(
            [d_q[:, :CHUNK], d_kv[:, : 2 * CHUNK], d_q[:, CHUNK:], d_kv[:, 2 * CHUNK :]], axis=1
        )
        d_normed = collect_z(nt_dot(d_qkv, wq))
        sums = jnp.sum(d_qkv.astype(jnp.float32), axis=0).reshape(2, 3, CHUNK)
        g_bqv = jnp.stack([sums[:, 0], sums[:, 2]])
        g_wout = lax.dot_general(
            low_full, mixed, (((0,), (0,)), ((), ())), preferred_element_type=jnp.float32
        )
        g_wqkv = lax.dot_general(
            normed_full, d_qkv, (((0,), (0,)), ((), ())), preferred_element_type=jnp.float32
        )
        attn_sum = core_sum(
            jnp.concatenate([g_wqkv.reshape(1024, 2, 384), g_wout.reshape(1024, 2, 128)], axis=2), core
        )
        d_x, g_g1, g_s1 = norm_pullback(resid_in, ln1_gain[at], ln1_bias[at], d_normed)
        grad = grad + d_x

        if at > 0:
            both = lax.psum_scatter(
                jnp.concatenate([attn_sum, feed_sum], axis=2), PLANE, scatter_dimension=0
            ).astype(jnp.float32)
            attn_out[at], feed_out[at] = both[:, : 4 * CHUNK], both[:, 4 * CHUNK :]
        else:
            feed_out[at] = lax.psum_scatter(feed_sum, PLANE, scatter_dimension=0).astype(jnp.float32)
            parts = lax.all_to_all(attn_sum, PLANE, 0, 0, tiled=True)
            attn_out[at] = jnp.sum(parts.astype(jnp.float32), axis=0)
        shared[at] = (g_bout, g_g1, g_s1, g_bdown, g_g2, g_s2)
        units[at] = (g_bqv, g_bup)
    hidden_grad = swap_rows(grad)

    early = jnp.stack([*shared[1], shared[0][0], *shared[0][3:]])
    early = jnp.sum(share(early, "z", 4), axis=0)
    unit_rows = jnp.concatenate(
        [
            jnp.stack([units[0][1], units[1][1]]),
            jnp.stack([units[0][0].reshape(512), units[1][0].reshape(512)]).reshape(1, 1024),
        ]
    )
    early = jnp.concatenate([early, unit_rows], axis=0)
    early = jnp.sum(share(early, PLANE_CORES, 32), axis=0)
    late = jnp.stack([shared[0][1], shared[0][2]])
    late = jnp.sum(share(late, "z", 4), axis=0)
    late = jnp.sum(share(late, PLANE_CORES, 32), axis=0)

    sum_bout = jnp.stack([early[6], early[0]])
    sum_g1 = jnp.stack([late[0], early[1]])
    sum_s1 = jnp.stack([late[1], early[2]])
    sum_bdown = jnp.stack([early[7], early[3]])
    sum_g2 = jnp.stack([early[8], early[4]])
    sum_s2 = jnp.stack([early[9], early[5]])
    sum_bup = lax.dynamic_index_in_dim(early[10:12].reshape(2, 2, 512), lane, 1, False)
    sum_bqv = lax.dynamic_index_in_dim(early[12].reshape(2, 2, 2, CHUNK), lane, 2, False)

    grad_w_qkv = jnp.stack([attn_out[at][:, :384].reshape(64, 3, CHUNK) for at in range(layer_count)])
    grad_w_out = jnp.stack([attn_out[at][:, 384:].T for at in range(layer_count)])
    grad_w_up = jnp.stack([feed_out[at][:, :512] for at in range(layer_count)])
    grad_w_down = jnp.stack([feed_out[at][:, 512:].T for at in range(layer_count)])
    return (
        hidden_out,
        hidden_grad,
        grad_w_qkv,
        sum_bqv,
        grad_w_out,
        sum_bout,
        sum_g1,
        sum_s1,
        grad_w_up,
        sum_bup,
        grad_w_down,
        sum_bdown,
        sum_g2,
        sum_s2,
    )


def solution(mesh):
    inner = Mesh(mesh.devices.reshape(2, 4, 2, 4, 2), AXES)
    dp = ("xh", "y", "c")
    tensor = ("z", "xl")
    rows = dp + tensor
    in_specs = (
        P(rows, None),
        P(rows),
        P(None, dp, None, tensor),
        P(None, None, tensor),
        P(None, tensor, dp),
        P(),
        P(),
        P(),
        P(None, dp, tensor),
        P(None, tensor),
        P(None, tensor, dp),
        P(),
        P(),
        P(),
        P(rows, None),
    )
    out_specs = (
        P(rows, None),
        P(rows, None),
        P(None, dp, None, tensor),
        P(None, None, tensor),
        P(None, tensor, dp),
        P(),
        P(),
        P(),
        P(None, dp, tensor),
        P(None, tensor),
        P(None, tensor, dp),
        P(),
        P(),
        P(),
    )
    return jax.shard_map(local, mesh=inner, in_specs=in_specs, out_specs=out_specs, check_vma=False)
```

time: 1720 us -> 739 us (0.43)
  waiting for transfers between devices: 1260 us -> 241 us
  blocking collectives: 226 us -> 0 us
  starting transfers between devices: 2.52 us -> 154 us
  local copies, waits for them, and re-layouts: 35.8 us -> 141 us
  matrix products: 115 us -> 69.9 us
  other arithmetic: 61.4 us -> 87 us
  Pallas kernels: 0 us -> 22.1 us
    reduce_scatter x16 -> x2, waiting for transfers between devices: 885 us -> 0.04 us  [the longest x1 0.02 us: local(): lax.psum_scatter(jnp.concatenate([attn_sum, feed_sum], axis=2), PLANE, sc...]
    all_gather x12 -> x1, waiting for transfers between devices: 368 us -> 0.02 us  [plane_gather(): return lax.all_gather(slab, PLANE, axis=0)]
    all_to_all x0 -> x24, waiting for transfers between devices: none -> 194 us  [the longest x15 114 us: share(): return lax.all_to_all(copies, axis, 0, 0, tiled=True)]
    all_gather x5 -> x0, blocking collectives: 124 us -> none  [the longest x2 62.8 us: local(): lax.all_gather(w_qkv[layer_at], 'dp', axis=0, tiled=True)]
    all_to_all x0 -> x24, starting transfers between devices: none -> 122 us  [the longest x15 81 us: share(): return lax.all_to_all(copies, axis, 0, 0, tiled=True)]
    psum x2 -> x0, blocking collectives: 101 us -> none  [the longest x1 65.2 us: local(): lax.psum(shared_stack, ('dp', 'tensor'))]
    ppermute x0 -> x17, waiting for transfers between devices: none -> 47.7 us  [the longest x4 47.7 us: swap_rows(): return lax.ppermute(values, ('c', 'xl'), [(0, 0), (1, 2), (2, 1), (3, 3)])]
    dot_general x48 -> x24, matrix products: 115 us -> 69.9 us  [the longest x8 30 us: nn_dot(): return jnp.dot(left, right, preferred_element_type=jnp.float32)]
  transfers between devices with their start and end apart: 28 -> 44, of which waited for: 24 -> 22; matrix products, arithmetic and copies ran while one was open for 5% -> 34% of each run, Pallas kernels for 0% -> 2%
where the time goes in v1:
time: 739 us; the launch traced here: 731 us
  waiting for transfers between devices  241 us (33%)
  starting transfers between devices  154 us (21%)
  local copies, waits for them, and re-layouts  141 us (19%)
  other arithmetic  87 us (12%)
  matrix products  69.9 us (9%)
  Pallas kernels  22.1 us (3%)
  between operations  15.5 us (2%)
    all_to_all x15, waiting for transfers between devices, share(): return lax.all_to_all(copies, axis, 0, 0, tiled=True)  114 us
    all_to_all x15, starting transfers between devices, share(): return lax.all_to_all(copies, axis, 0, 0, tiled=True)  81 us
    all_to_all x8, waiting for transfers between devices, collect_z(): arrived = lax.all_to_all(chunks, 'z', 0, 0, tiled=True)  63.3 us
    ppermute x4, waiting for transfers between devices, swap_rows(): return lax.ppermute(values, ('c', 'xl'), [(0, 0), (1, 2), (2, 1), (3, 3)])  47.7 us
    all_to_all x8, starting transfers between devices, collect_z(): arrived = lax.all_to_all(chunks, 'z', 0, 0, tiled=True)  34.5 us
    dot_general x8, matrix products, nn_dot(): return jnp.dot(left, right, preferred_element_type=jnp.float32)  30 us
    concatenate x2, local copies, waits for them, and re-layouts, local(): jnp.concatenate([g_wup.reshape(1024, 2, 512), g_wdown.reshape(1024, 2, 51...  19.5 us
    broadcast_in_dim x15, local copies, waits for them, and re-layouts, share(): copies = jnp.broadcast_to(values[None], (count,) + values.shape)  18.8 us
  transfers between devices with their start and end apart: 44, of which 22 were waited for; matrix products, arithmetic and copies ran while one was open for 34% of the time, Pallas kernels for 2%

profile of v1, /device:TPU:1, one launch (start us, length us, event | category | flops | bytes accessed | tf_op | source)
XLA Modules:
  0.0 730.9 jit_solution(6881403093214978122)
XLA Ops:
  18.9 6.8 all-to-all-start.1
  26.4 28.0 %all-to-all-done.1 = bf16[16,64,512]{2,1,0:T(8,128)(2,1)S(1)} async-done(((bf16[16,64,512]{2,1,0:T(8,128)(2,1)}), bf16[16,64,512]{2,1,0:T(8,128)(2,1)S(1)}, u32[]{:S(2)}, u32[]{:S(2)}) %all-to-all-start.1) | async-done | bytes 1048608 | tf_op jit(solution)/shard_map/all_to_all | solution.py:40
  55.1 5.8 all-to-all-start.2
  61.4 4.8 all-to-all-done.2
  70.9 14.4 %all-to-all-done = bf16[4,128,1024]{1,2,0:T(8,128)(2,1)S(1)} async-done(((bf16[4,128,1024]{1,2,0:T(8,128)(2,1)}), bf16[4,128,1024]{1,2,0:T(8,128)(2,1)S(1)}, u32[]{:S(2)}, u32[]{:S(2)}) %all-to-all-start) | async-done | bytes 1048608 | tf_op jit(solution)/shard_map/all_to_all | solution.py:40
  102.3 25.9 %all-to-all-done.5 = bf16[16,64,1024]{2,1,0:T(8,128)(2,1)} async-done(((bf16[16,64,1024]{2,1,0:T(8,128)(2,1)}), bf16[16,64,1024]{2,1,0:T(8,128)(2,1)}, u32[]{:S(2)}, u32[]{:S(2)}) %all-to-all-start.5) | async-done | bytes 2097184 | tf_op jit(solution)/shard_map/all_to_all | solution.py:40
  140.8 14.9 %all-to-all-done.3 = bf16[4,128,1024]{2,1,0:T(8,128)(2,1)S(1)} async-done(((bf16[4,128,1024]{2,1,0:T(8,128)(2,1)}), bf16[4,128,1024]{2,1,0:T(8,128)(2,1)S(1)}, u32[]{:S(2)}, u32[]{:S(2)}) %all-to-all-start.3) | async-done | bytes 1048608 | tf_op jit(solution)/shard_map/all_to_all | solution.py:50
  157.8 14.9 %all-to-all-start.4 = ((bf16[4,128,1024]{1,2,0:T(8,128)(2,1)}), bf16[4,128,1024]{1,2,0:T(8,128)(2,1)}, u32[]{:S(2)}, u32[]{:S(2)}) async-start(bf16[4,128,1024]{1,2,0:T(8,128)(2,1)} %broadcast_in_dim.58), calls=%async_computation.4 | async-start | bytes 2097152 | tf_op jit(solution)/shard_map/all_to_all | solution.py:40
  199.1 13.3 %all-to-all-done.6 = bf16[4,128,1024]{2,1,0:T(8,128)(2,1)} async-done(((bf16[4,128,1024]{2,1,0:T(8,128)(2,1)}), bf16[4,128,1024]{2,1,0:T(8,128)(2,1)}, u32[]{:S(2)}, u32[]{:S(2)}) %all-to-all-start.6) | async-done | bytes 1048608 | tf_op jit(solution)/shard_map/all_to_all | solution.py:50
  224.4 15.2 %all-to-all-done.7 = bf16[4,128,1024]{1,2,0:T(8,128)(2,1)S(1)} async-done(((bf16[4,128,1024]{1,2,0:T(8,128)(2,1)}), bf16[4,128,1024]{1,2,0:T(8,128)(2,1)S(1)}, u32[]{:S(2)}, u32[]{:S(2)}) %all-to-all-start.7) | async-done | bytes 1048608 | tf_op jit(solution)/shard_map/all_to_all | solution.py:40
  259.8 5.3 attend_forward.3
  279.6 5.9 all-to-all-done.8
  298.0 7.7 %all-to-all-done.11 = bf16[4,128,1024]{2,1,0:T(8,128)(2,1)} async-done(((bf16[4,128,1024]{2,1,0:T(8,128)(2,1)}), bf16[4,128,1024]{2,1,0:T(8,128)(2,1)}, u32[]{:S(2)}, u32[]{:S(2)}) %all-to-all-start.11) | async-done | bytes 1048608 | tf_op jit(solution)/shard_map/all_to_all | solution.py:40
  332.8 6.6 convert_reduce_fusion.8
  350.6 7.3 %all-to-all-done.12 = bf16[4,128,1024]{2,1,0:T(8,128)(2,1)} async-done(((bf16[4,128,1024]{2,1,0:T(8,128)(2,1)}), bf16[4,128,1024]{2,1,0:T(8,128)(2,1)}, u32[]{:S(2)}, u32[]{:S(2)}) %all-to-all-start.12) | async-done | bytes 1048608 | tf_op jit(solution)/shard_map/all_to_all | solution.py:50
  368.3 4.8 all-to-all-done.10
  394.5 4.9 convert_bitcast_fusion.4
  399.4 8.8 %reshape.651 = bf16[8,2,64,2,512]{2,1,0,4,3:T(2,128)(2,1)} reshape(bf16[1024,1024]{0,1:T(8,128)(2,1)} %convert_bitcast_fusion.4) | data formatting | bytes 4194304 | tf_op jit(solution)/shard_map/concatenate | solution.py:359
  408.2 10.7 %copy.294 = bf16[8,2,64,2,512]{4,2,3,1,0:T(8,128)(2,1)} copy(bf16[8,2,64,2,512]{2,1,0,4,3:T(2,128)(2,1)} %reshape.651) | data formatting | bytes 4194304 | tf_op jit(solution)/shard_map/concatenate | solution.py:359
  423.0 6.5 attend_backward.2
  429.5 5.6 collective-permute-start.10
  489.3 6.4 convert_reduce_fusion.9
  509.2 7.2 all-to-all-done.16
  542.8 6.1 attend_backward.3
  579.7 10.0 %all-to-all-done.18 = bf16[4,128,1024]{2,1,0:T(8,128)(2,1)} async-done(((bf16[4,128,1024]{2,1,0:T(8,128)(2,1)}), bf16[4,128,1024]{2,1,0:T(8,128)(2,1)}, u32[]{:S(2)}, u32[]{:S(2)}) %all-to-all-start.18) | async-done | bytes 1048608 | tf_op jit(solution)/shard_map/all_to_all | solution.py:50
  600.9 7.7 %all-to-all-start.23 = ((f32[32,2,1024]{2,1,0:T(2,128)}), f32[32,2,1024]{2,1,0:T(2,128)S(1)}, u32[]{:S(2)}, u32[]{:S(2)}) async-start(f32[32,2,1024]{2,1,0:T(2,128)} %broadcast_in_dim.77), calls=%async_computation.24 | async-start | bytes 524288 | tf_op jit(solution)/shard_map/all_to_all | solution.py:40
  610.0 7.2 all-to-all-done.23
  618.7 5.5 all-to-all-start.21
  636.3 33.5 %collective-permute-done.8 = bf16[128,1024]{1,0:T(8,128)(2,1)} collective-permute-done((bf16[128,1024]{1,0:T(8,128)(2,1)}, bf16[128,1024]{1,0:T(8,128)(2,1)}, u32[]{:S(2)}, u32[]{:S(2)}) %collective-permute-start.8) | collective-permute-done | bytes 262176 | tf_op jit(solution)/shard_map/ppermute | solution.py:31
  672.5 14.0 %collective-permute-done.12 = f32[128,1024]{1,0:T(8,128)S(1)} collective-permute-done((f32[128,1024]{1,0:T(8,128)}, f32[128,1024]{1,0:T(8,128)S(1)}, u32[]{:S(2)}, u32[]{:S(2)}) %collective-permute-start.12) | collective-permute-done | bytes 524320 | tf_op jit(solution)/shard_map/ppermute | solution.py:31
  686.5 6.9 all-to-all-start.19
  700.0 16.5 %all-to-all-done.19 = bf16[16,64,512]{2,1,0:T(8,128)(2,1)S(1)} async-done(((bf16[16,64,512]{2,1,0:T(8,128)(2,1)}), bf16[16,64,512]{2,1,0:T(8,128)(2,1)S(1)}, u32[]{:S(2)}, u32[]{:S(2)}) %all-to-all-start.19) | async-done | bytes 1048608 | tf_op jit(solution)/shard_map/all_to_all | solution.py:395
  (430 shorter events, 376.3 us)
Async XLA Ops:
  7.2 207.1 %all-gather.3.cloned.1.call-start = ((), (), s32[]{:S(2)}) async-start(), calls=%async_computation.28 | async-start | bytes 3342336 | tf_op jit(solution)/shard_map/all_gather | solution.py:273
  8.6 62.2 %collective-permute-start.2 = (f32[2,768]{1,0:T(2,128)S(1)}, f32[2,768]{1,0:T(2,128)S(1)}, u32[]{:S(2)}, u32[]{:S(2)}) collective-permute-start(f32[2,768]{1,0:T(2,128)S(1)} %constant_dynamic-update-slice_fusion), channel_id=1, source_target_pairs={{0,1},{1,0},{2,3},{3,2},{4,5},{5,4},{6,7},{7,6},{8,9},{9,8},{10,11... | collective-permute-start | bytes 18440 | tf_op jit(solution)/shard_map/ppermute | solution.py:297
  18.9 35.6 %all-to-all-start.1 = ((bf16[16,64,512]{2,1,0:T(8,128)(2,1)}), bf16[16,64,512]{2,1,0:T(8,128)(2,1)S(1)}, u32[]{:S(2)}, u32[]{:S(2)}) async-start(bf16[16,64,512]{2,1,0:T(8,128)(2,1)} %broadcast_in_dim.53), calls=%async_computation.1 | async-start | bytes 2097152 | tf_op jit(solution)/shard_map/all_to_all | solution.py:40
  61.2 31.5 %collective-permute-start.1 = (bf16[16,64,512]{2,1,0:T(8,128)(2,1)S(1)}, bf16[16,64,512]{2,1,0:T(8,128)(2,1)}, u32[]{:S(2)}, u32[]{:S(2)}) collective-permute-start(bf16[16,64,512]{2,1,0:T(8,128)(2,1)S(1)} %all-to-all-done.1), channel_id=1, source_target_pairs={{0,8},{8,0},{1,9},{9,1},{2,10},{10,2},{3,11},{11,3},{4,12},{12,4},... | collective-permute-start | bytes 3145736 | tf_op jit(solution)/shard_map/ppermute | solution.py:35
  67.3 18.0 %all-to-all-start = ((bf16[4,128,1024]{1,2,0:T(8,128)(2,1)}), bf16[4,128,1024]{1,2,0:T(8,128)(2,1)S(1)}, u32[]{:S(2)}, u32[]{:S(2)}) async-start(bf16[4,128,1024]{1,2,0:T(8,128)(2,1)} %broadcast_in_dim.52), calls=%async_computation | async-start | bytes 2097152 | tf_op jit(solution)/shard_map/all_to_all | solution.py:40
  86.9 41.3 %all-to-all-start.5 = ((bf16[16,64,1024]{2,1,0:T(8,128)(2,1)}), bf16[16,64,1024]{2,1,0:T(8,128)(2,1)}, u32[]{:S(2)}, u32[]{:S(2)}) async-start(bf16[16,64,1024]{2,1,0:T(8,128)(2,1)} %broadcast_in_dim.59), calls=%async_computation.5 | async-start | bytes 4194304 | tf_op jit(solution)/shard_map/all_to_all | solution.py:40
  100.6 30.0 %collective-permute-start.3 = (bf16[512,512]{1,0:T(8,128)(2,1)S(1)}, bf16[512,512]{1,0:T(8,128)(2,1)S(1)}, u32[]{:S(2)}, u32[]{:S(2)}) collective-permute-start(bf16[512,512]{1,0:T(8,128)(2,1)S(1)} %pad_maximum_fusion.3), channel_id=1, source_target_pairs={{0,8},{8,0},{1,9},{9,1},{2,10},{10,2},{3,11},{11,3},{4,12},{12,4},... | collective-permute-start | bytes 1572872 | tf_op jit(solution)/shard_map/ppermute | solution.py:35
  128.2 44.5 %collective-permute-start.4 = (bf16[16,64,1024]{2,1,0:T(8,128)(2,1)}, bf16[16,64,1024]{2,1,0:T(8,128)(2,1)}, u32[]{:S(2)}, u32[]{:S(2)}) collective-permute-start(bf16[16,64,1024]{2,1,0:T(8,128)(2,1)} %all-to-all-done.5), channel_id=1, source_target_pairs={{0,8},{8,0},{1,9},{9,1},{2,10},{10,2},{3,11},{11,3},{4,12},{12,4},... | collective-permute-start | bytes 6291464 | tf_op jit(solution)/shard_map/ppermute | solution.py:35
  136.6 19.1 %all-to-all-start.3 = ((bf16[4,128,1024]{2,1,0:T(8,128)(2,1)}), bf16[4,128,1024]{2,1,0:T(8,128)(2,1)S(1)}, u32[]{:S(2)}, u32[]{:S(2)}) async-start(bf16[4,128,1024]{2,1,0:T(8,128)(2,1)} %bitcast.449), calls=%async_computation.3 | async-start | bytes 2097152 | tf_op jit(solution)/shard_map/all_to_all | solution.py:50
  157.8 28.9 %all-to-all-start.4 = ((bf16[4,128,1024]{1,2,0:T(8,128)(2,1)}), bf16[4,128,1024]{1,2,0:T(8,128)(2,1)}, u32[]{:S(2)}, u32[]{:S(2)}) async-start(bf16[4,128,1024]{1,2,0:T(8,128)(2,1)} %broadcast_in_dim.58), calls=%async_computation.4 | async-start | bytes 2097152 | tf_op jit(solution)/shard_map/all_to_all | solution.py:40
  216.6 28.3 %collective-permute-start.5 = (bf16[16,64,512]{2,1,0:T(8,128)(2,1)}, bf16[16,64,512]{2,1,0:T(8,128)(2,1)}, u32[]{:S(2)}, u32[]{:S(2)}) collective-permute-start(bf16[16,64,512]{2,1,0:T(8,128)(2,1)} %slice.329), channel_id=1, source_target_pairs={{0,8},{8,0},{1,9},{9,1},{2,10},{10,2},{3,11},{11,3},{4,12},{12,4},... | collective-permute-start | bytes 3145736 | tf_op jit(solution)/shard_map/ppermute | solution.py:35
  220.8 18.8 %all-to-all-start.7 = ((bf16[4,128,1024]{1,2,0:T(8,128)(2,1)}), bf16[4,128,1024]{1,2,0:T(8,128)(2,1)S(1)}, u32[]{:S(2)}, u32[]{:S(2)}) async-start(bf16[4,128,1024]{1,2,0:T(8,128)(2,1)} %broadcast_in_dim.60), calls=%async_computation.7 | async-start | bytes 2097152 | tf_op jit(solution)/shard_map/all_to_all | solution.py:40
  244.1 30.9 %collective-permute-start.7 = (bf16[16,64,1024]{2,1,0:T(8,128)(2,1)}, bf16[16,64,1024]{2,1,0:T(8,128)(2,1)}, u32[]{:S(2)}, u32[]{:S(2)}) collective-permute-start(bf16[16,64,1024]{2,1,0:T(8,128)(2,1)} %slice.336), channel_id=1, source_target_pairs={{0,8},{8,0},{1,9},{9,1},{2,10},{10,2},{3,11},{11,3},{4,12},{12,4},... | collective-permute-start | bytes 6291464 | tf_op jit(solution)/shard_map/ppermute | solution.py:35
  266.5 19.0 %all-to-all-start.8 = ((bf16[4,128,1024]{2,1,0:T(8,128)(2,1)}), bf16[4,128,1024]{2,1,0:T(8,128)(2,1)}, u32[]{:S(2)}, u32[]{:S(2)}) async-start(bf16[4,128,1024]{2,1,0:T(8,128)(2,1)} %bitcast.448), calls=%async_computation.8 | async-start | bytes 2097152 | tf_op jit(solution)/shard_map/all_to_all | solution.py:50
  287.6 18.1 %all-to-all-start.11 = ((bf16[4,128,1024]{2,1,0:T(8,128)(2,1)}), bf16[4,128,1024]{2,1,0:T(8,128)(2,1)}, u32[]{:S(2)}, u32[]{:S(2)}) async-start(bf16[4,128,1024]{2,1,0:T(8,128)(2,1)} %broadcast_in_dim.62), calls=%async_computation.11 | async-start | bytes 2097152 | tf_op jit(solution)/shard_map/all_to_all | solution.py:40
  307.7 22.8 %all-to-all-start.9 = ((bf16[4,128,1024]{1,2,0:T(8,128)(2,1)}), bf16[4,128,1024]{1,2,0:T(8,128)(2,1)}, u32[]{:S(2)}, u32[]{:S(2)}) async-start(bf16[4,128,1024]{1,2,0:T(8,128)(2,1)} %broadcast_in_dim.61), calls=%async_computation.9 | async-start | bytes 2097152 | tf_op jit(solution)/shard_map/all_to_all | solution.py:40
  383.1 35.8 %all-to-all-start.13 = ((bf16[4,128,1024]{1,2,0:T(8,128)(2,1)}), bf16[4,128,1024]{1,2,0:T(8,128)(2,1)}, u32[]{:S(2)}, u32[]{:S(2)}) async-start(bf16[4,128,1024]{1,2,0:T(8,128)(2,1)} %broadcast_in_dim.65), calls=%async_computation.13 | async-start | bytes 2097152 | tf_op jit(solution)/shard_map/all_to_all | solution.py:40
  441.2 20.6 %all-to-all-start.14 = ((bf16[4,128,1024]{2,1,0:T(8,128)(2,1)}), bf16[4,128,1024]{2,1,0:T(8,128)(2,1)}, u32[]{:S(2)}, u32[]{:S(2)}) async-start(bf16[4,128,1024]{2,1,0:T(8,128)(2,1)} %bitcast.496), calls=%async_computation.14 | async-start | bytes 2097152 | tf_op jit(solution)/shard_map/all_to_all | solution.py:50
  448.9 23.1 %collective-permute-start.15 = (bf16[8,2,64,1024]{3,2,1,0:T(8,128)(2,1)}, bf16[8,2,64,1024]{3,2,1,0:T(8,128)(2,1)}, u32[]{:S(2)}, u32[]{:S(2)}) collective-permute-start(bf16[8,2,64,1024]{3,2,1,0:T(8,128)(2,1)} %fusion.37), channel_id=1, source_target_pairs={{0,8},{8,0},{1,9},{9,1},{2,10},{10,2},{3,11},{11,3},{4,12},{12,4},... | collective-permute-start | bytes 6291464 | tf_op jit(solution)/shard_map/ppermute | solution.py:35
  467.4 19.6 %all-to-all-start.15 = ((bf16[4,128,1024]{1,2,0:T(8,128)(2,1)}), bf16[4,128,1024]{1,2,0:T(8,128)(2,1)}, u32[]{:S(2)}, u32[]{:S(2)}) async-start(bf16[4,128,1024]{1,2,0:T(8,128)(2,1)} %broadcast_in_dim.68), calls=%async_computation.15 | async-start | bytes 2097152 | tf_op jit(solution)/shard_map/all_to_all | solution.py:40
  484.6 18.1 %collective-permute-start.14 = (bf16[8,2,64,512]{3,2,1,0:T(8,128)(2,1)}, bf16[8,2,64,512]{3,2,1,0:T(8,128)(2,1)}, u32[]{:S(2)}, u32[]{:S(2)}) collective-permute-start(bf16[8,2,64,512]{3,2,1,0:T(8,128)(2,1)} %fusion.54), channel_id=1, source_target_pairs={{0,8},{8,0},{1,9},{9,1},{2,10},{10,2},{3,11},{11,3},{4,12},{12,4},... | collective-permute-start | bytes 3145736 | tf_op jit(solution)/shard_map/ppermute | solution.py:35
  498.0 18.3 %all-to-all-start.16 = ((bf16[4,128,1024]{2,1,0:T(8,128)(2,1)}), bf16[4,128,1024]{2,1,0:T(8,128)(2,1)}, u32[]{:S(2)}, u32[]{:S(2)}) async-start(bf16[4,128,1024]{2,1,0:T(8,128)(2,1)} %bitcast.493), calls=%async_computation.16 | async-start | bytes 2097152 | tf_op jit(solution)/shard_map/all_to_all | solution.py:50
  502.2 214.6 %reduce-scatter.3.cloned.1.call-start = ((), (), s32[]{:S(2)}) async-start(), calls=%async_computation.26 | async-start | bytes 3342336 | tf_op jit(solution)/shard_map/reduce_scatter | solution.py:389
  548.9 18.3 %collective-permute-start.11 = (bf16[512,512]{1,0:T(8,128)(2,1)}, bf16[512,512]{1,0:T(8,128)(2,1)}, u32[]{:S(2)}, u32[]{:S(2)}) collective-permute-start(bf16[512,512]{1,0:T(8,128)(2,1)} %get-tuple-element.33), channel_id=1, source_target_pairs={{0,8},{8,0},{1,9},{9,1},{2,10},{10,2},{3,11},{11,3},{4,12},{12,4},... | collective-permute-start | bytes 1572872 | tf_op jit(solution)/shard_map/ppermute | solution.py:35
  562.0 62.3 %collective-permute-start.16 = (bf16[8,2,64,1024]{3,2,1,0:T(8,128)(2,1)}, bf16[8,2,64,1024]{3,2,1,0:T(8,128)(2,1)}, u32[]{:S(2)}, u32[]{:S(2)}) collective-permute-start(bf16[8,2,64,1024]{3,2,1,0:T(8,128)(2,1)} %fusion.33), channel_id=1, source_target_pairs={{0,8},{8,0},{1,9},{9,1},{2,10},{10,2},{3,11},{11,3},{4,12},{12,4},... | collective-permute-start | bytes 6291464 | tf_op jit(solution)/shard_map/ppermute | solution.py:35
  570.8 18.8 %all-to-all-start.18 = ((bf16[4,128,1024]{2,1,0:T(8,128)(2,1)}), bf16[4,128,1024]{2,1,0:T(8,128)(2,1)}, u32[]{:S(2)}, u32[]{:S(2)}) async-start(bf16[4,128,1024]{2,1,0:T(8,128)(2,1)} %bitcast.497), calls=%async_computation.18 | async-start | bytes 2097152 | tf_op jit(solution)/shard_map/all_to_all | solution.py:50
  609.8 60.1 %collective-permute-start.13 = (bf16[8,2,64,512]{3,2,1,0:T(8,128)(2,1)}, bf16[8,2,64,512]{3,2,1,0:T(8,128)(2,1)}, u32[]{:S(2)}, u32[]{:S(2)}) collective-permute-start(bf16[8,2,64,512]{3,2,1,0:T(8,128)(2,1)} %fusion.58), channel_id=1, source_target_pairs={{0,8},{8,0},{1,9},{9,1},{2,10},{10,2},{3,11},{11,3},{4,12},{12,4},... | collective-permute-start | bytes 3145736 | tf_op jit(solution)/shard_map/ppermute | solution.py:35
  618.7 67.7 %all-to-all-start.21 = ((f32[32,13,1024]{2,1,0:T(8,128)}), f32[32,13,1024]{2,1,0:T(8,128)}, u32[]{:S(2)}, u32[]{:S(2)}) async-start(f32[32,13,1024]{2,1,0:T(8,128)} %broadcast_in_dim.75), calls=%async_computation.22 | async-start | bytes 4194304 | tf_op jit(solution)/shard_map/all_to_all | solution.py:40
  624.3 95.0 %reduce-scatter.5.cloned.1.call-start = ((), (), s32[]{:S(2)}) async-start(), calls=%async_computation.27 | async-start | bytes 2228224 | tf_op jit(solution)/shard_map/reduce_scatter | solution.py:394
  628.4 41.5 %collective-permute-start.8 = (bf16[128,1024]{1,0:T(8,128)(2,1)}, bf16[128,1024]{1,0:T(8,128)(2,1)}, u32[]{:S(2)}, u32[]{:S(2)}) collective-permute-start(bf16[128,1024]{1,0:T(8,128)(2,1)} %get-tuple-element.179), channel_id=1, source_target_pairs={{0,0},{1,8},{8,1},{9,9},{2,2},{3,10},{10,3},{11,11},{4,4},{5,12},{... | collective-permute-start | bytes 786440 | tf_op jit(solution)/shard_map/ppermute | solution.py:31
  634.3 52.1 %collective-permute-start.12 = (f32[128,1024]{1,0:T(8,128)}, f32[128,1024]{1,0:T(8,128)S(1)}, u32[]{:S(2)}, u32[]{:S(2)}) collective-permute-start(f32[128,1024]{1,0:T(8,128)} %add_add_fusion.4), channel_id=1, source_target_pairs={{0,0},{1,8},{8,1},{9,9},{2,2},{3,10},{10,3},{11,11},{4,4},{5,12},{... | collective-permute-start | bytes 1572872 | tf_op jit(solution)/shard_map/ppermute | solution.py:31
  686.5 30.1 %all-to-all-start.19 = ((bf16[16,64,512]{2,1,0:T(8,128)(2,1)}), bf16[16,64,512]{2,1,0:T(8,128)(2,1)S(1)}, u32[]{:S(2)}, u32[]{:S(2)}) async-start(bf16[16,64,512]{2,1,0:T(8,128)(2,1)} %bitcast.446), calls=%async_computation.19 | async-start | bytes 2097152 | tf_op jit(solution)/shard_map/all_to_all | solution.py:395
  (66 other events, 614.3 us)
Sparse Core Ops, SparseCore 0:
  14.9 96.6 all-gather.2
  506.9 73.3 reduce-scatter.2
  628.5 83.2 reduce-scatter.4
